TPU v7x, 32 devices: a whole 2x2x4 slice. The times are simulated.
32 devices in a mesh: groups: 2 (over y), blk: 4 (over z), panel: 4 (over x, core).
Axes of the slice: x: 2, y: 2, z: 4, core: 2. Of those that a mesh axis runs over, the one named last changes fastest.
Arguments:
- points: bfloat16 [4096, 256], P(('groups', 'blk', 'panel')), parts along dimension 0, may hold values from -6 to 6
- targets: float32 [4096, 64], P(('groups', 'blk', 'panel')), parts along dimension 0, may hold values from -6 to 6
Outputs:
- solution: float32 [4096, 64], P(('groups', 'blk', 'panel')), parts along dimension 0
- residual: float32 [4096, 64], P(('groups', 'blk', 'panel')), parts along dimension 0
- direction: float32 [4096, 64], P(('groups', 'blk', 'panel')), parts along dimension 0
There are 2 independent parts, one for each index of `groups`. A program takes and returns all parts, laid end to end along the dimension named above; each array names one. Nothing has to cross between parts.
All inputs are finite; a program needn't handle non-finite values.
Results may differ from a plain program's by a relative error of at most 0.001.
The roundings to bfloat16 on the way count: a program that leaves them out, or rounds other values in their place, can miss the bound.
Values may be sent and summed in bfloat16 or wider, within the bound.
A program may use at most 64 MiB of HBM per device.

v0:
```python
import jax
import jax.numpy as jnp
from jax import lax
from jax.sharding import PartitionSpec as P


def kernel_tile(query, sq_query, keys, sq_keys, ell2):
    cross = jnp.einsum("qd,kd->qk", query, keys, preferred_element_type=jnp.float32)
    dist = jnp.maximum(sq_query[:, None] + sq_keys[None, :] - 2.0 * cross, 0.0)
    return jnp.exp(-dist / (2.0 * ell2)).astype(jnp.bfloat16)


def square_norms(values):
    wide = values.astype(jnp.float32)
    return jnp.sum(wide * wide, axis=1)


def local_terms(queries, sq_queries, keys, dir_piece, ell2):
    sq_keys = square_norms(keys)
    rows = queries.shape[0]
    block_rows = 512
    count = rows // block_rows
    query_blocks = queries.reshape(count, block_rows, queries.shape[1])
    sq_blocks = sq_queries.reshape(count, block_rows)

    def one_block(pair):
        tile = kernel_tile(pair[0], pair[1], keys, sq_keys, ell2)
        return jnp.dot(tile, dir_piece, preferred_element_type=jnp.float32)

    return lax.map(one_block, (query_blocks, sq_blocks)).reshape(rows, dir_piece.shape[1])


def solve_spd(matrix, right):
    return jax.scipy.linalg.cho_solve((jnp.linalg.cholesky(matrix), True), right)


def local(points, targets):
    highest = lax.Precision.HIGHEST
    ell2 = points.shape[1] / 4.0
    dir_low = targets.astype(jnp.bfloat16)
    queries = lax.all_gather(points, "panel", axis=0, tiled=True)
    sq_queries = square_norms(queries)
    partial_value = local_terms(
        queries,
        sq_queries,
        lax.all_gather(points, "blk", axis=0, tiled=True),
        lax.all_gather(dir_low, "blk", axis=0, tiled=True),
        ell2,
    )
    products = lax.psum_scatter(partial_value, "panel", scatter_dimension=0, tiled=True)
    image = 1.0 * targets + products
    local_gram = jnp.dot(targets.T, targets, precision=highest)
    local_curv = jnp.dot(targets.T, image, precision=highest)
    local_quad = jnp.dot(image.T, image, precision=highest)
    gram, curv, quad = lax.psum((local_gram, local_curv, local_quad), ("blk", "panel"))
    alpha = solve_spd(curv, gram)
    solution = jnp.dot(targets, alpha, precision=highest)
    residual = targets - jnp.dot(image, alpha, precision=highest)
    cross_term = jnp.dot(curv, alpha, precision=highest)
    newgram = (
        gram
        - cross_term.T
        - cross_term
        + jnp.dot(alpha.T, jnp.dot(quad, alpha, precision=highest), precision=highest)
    )
    beta = solve_spd(gram, newgram)
    direction = residual + jnp.dot(targets, beta, precision=highest)
    return (solution, residual, direction)


def solution(mesh):
    placed = (P(("groups", "blk", "panel"), None), P(("groups", "blk", "panel"), None))
    return jax.shard_map(
        local,
        mesh=mesh,
        in_specs=placed,
        out_specs=(
            P(("groups", "blk", "panel"), None),
            P(("groups", "blk", "panel"), None),
            P(("groups", "blk", "panel"), None),
        ),
        check_vma=False,
    )
```

profile of v0, /device:TPU:0, one launch (start us, length us, event | category | flops | bytes accessed | tf_op | source)
XLA Modules:
  0.0 159.7 jit_solution(5839104339084445046)
XLA Ops:
  7.2 0.0 copy-start.1
  7.2 0.0 reduce-scatter.2.cloned.1.call-start
  7.2 15.8 %all_gather.10 = bf16[512,256]{1,0:T(8,128)(2,1)S(1)} all-gather(bf16[128,256]{1,0:T(8,128)(2,1)} %param.5), channel_id=1, replica_groups=mesh['groups'=2,'blk'=4,'panel'=4] {'blk'}, dimensions={0}, use_global_device_ids=true | all-gather | bytes 327680 | tf_op jit(solution)/shard_map/all_gather | solution.py:46
  23.1 0.0 copy-done.1
  23.1 5.8 %all_gather.9 = bf16[512,256]{1,0:T(8,128)(2,1)S(1)} all-gather(bf16[128,256]{1,0:T(8,128)(2,1)S(1)} %copy-done.1), channel_id=1, replica_groups=mesh['groups'=2,'blk'=4,'panel'=4] {'panel'}, dimensions={0}, use_global_device_ids=true | all-gather | bytes 327680 | tf_op jit(solution)/shard_map/all_gather | solution.py:41
  28.8 0.1 multiply_reduce_fusion
  29.0 0.0 copy-start
  29.0 0.1 multiply_reduce_fusion.1
  29.2 0.6 copy-done
  29.8 12.1 %all_gather.11 = bf16[512,64]{0,1:T(8,128)(2,1)S(1)} all-gather(bf16[128,64]{0,1:T(8,128)(2,1)S(1)} %convert_element_type.16), channel_id=1, replica_groups=mesh['groups'=2,'blk'=4,'panel'=4] {'blk'}, dimensions={0}, use_global_device_ids=true | all-gather | bytes 81920 | tf_op jit(solution)/shard_map/all_gather | solution.py:47
  41.8 1.3 fusion.6
  43.1 0.0 reduce-scatter.2.cloned.1.call-update
  43.1 0.2 fusion.30
  43.3 19.8 %reduce-scatter.2.cloned.1.call-done = f32[128,64]{0,1:T(8,128)} async-done(((f32[512,64]{0,1:T(8,128)}), f32[128,64]{0,1:T(8,128)}) %reduce-scatter.2.cloned.1.call-update) | async-done | bytes 32784 | tf_op jit(solution)/shard_map/reduce_scatter | solution.py:50
  63.1 0.8 add.53
  63.9 0.2 convolution_bitcast_fusion.2
  64.1 0.2 fusion.32
  64.3 60.6 %all-reduce = (f32[64,64]{0,1:T(8,128)S(1)}, f32[64,64]{0,1:T(8,128)S(1)}, f32[64,64]{1,0:T(8,128)S(1)}) all-reduce(f32[64,64]{0,1:T(8,128)S(1)} %fusion.30, f32[64,64]{0,1:T(8,128)S(1)} %convolution_bitcast_fusion.2, f32[64,64]{1,0:T(8,128)S(1)} %fusion.32), channel_id=1, replica_groups=mesh['groups'=2,'blk'=4,'panel'=4] {'blk','panel'}, use_global_device_ids=true, to_apply=%region_6.8 | all-reduce | flops 12288 | bytes 98304 | tf_op jit(solution)/shard_map/psum | solution.py:55
  124.9 0.1 copy.7
  125.0 0.1 copy.5
  125.1 5.8 %cholesky.44 = f32[64,64]{1,0:T(8,128)S(1)} custom-call(f32[64,64]{1,0:T(8,128)S(1)} %get-tuple-element.30), custom_call_target="Cholesky" | custom-call | tf_op jit(solution)/shard_map/jit(cholesky)/cholesky | solution.py:34
  131.0 0.6 compare_reduce_fusion.1
  131.6 0.7 fusion.14
  132.3 4.9 %custom-call.8 = f32[1,64,64]{1,2,0:T(8,128)S(1)} custom-call(f32[1,64,64]{2,1,0:T(8,128)S(1)} %fusion.14), custom_call_target="InvertDiagBlocksLowerTriangular" | custom-call | tf_op jit(solution)/shard_map/jit(_cho_solve)/triangular_solve | solution.py:34
  137.2 0.2 fusion.24
  137.4 0.2 fusion.22
  137.6 0.2 fusion.31
  137.8 0.2 convolution_subtract_fusion
  138.1 0.0 copy-start.2
  138.1 0.9 convolution_bitcast_fusion.1
  139.0 5.8 %cholesky.55 = f32[64,64]{1,0:T(8,128)S(1)} custom-call(f32[64,64]{1,0:T(8,128)S(1)} %get-tuple-element.29), custom_call_target="Cholesky" | custom-call | tf_op jit(solution)/shard_map/jit(cholesky)/cholesky | solution.py:34
  144.8 0.6 compare_reduce_fusion
  145.5 0.7 fusion.15
  146.1 4.9 %custom-call.9 = f32[1,64,64]{1,2,0:T(8,128)S(1)} custom-call(f32[1,64,64]{2,1,0:T(8,128)S(1)} %fusion.15), custom_call_target="InvertDiagBlocksLowerTriangular" | custom-call | tf_op jit(solution)/shard_map/jit(_cho_solve)/triangular_solve | solution.py:34
  151.0 0.1 copy.8
  151.1 0.2 fusion.33
  151.3 0.2 convolution_add_fusion
  151.6 0.2 fusion.19
  151.8 0.2 fusion.17
  152.0 0.0 copy-done.2
  152.0 0.9 fusion.7
  (4 shorter events, 0.1 us)
Async XLA Ops:
  7.2 15.9 %copy-start.1 = (bf16[128,256]{1,0:T(8,128)(2,1)S(1)}, bf16[128,256]{1,0:T(8,128)(2,1)}, u32[]{:S(2)}) copy-start(bf16[128,256]{1,0:T(8,128)(2,1)} %param.5) | copy-start | bytes 196612
  7.2 55.9 %reduce-scatter.2.cloned.1.call-start = ((), (), s32[]{:S(2)}) async-start(), calls=%async_computation.1 | async-start | bytes 163840 | tf_op jit(solution)/shard_map/reduce_scatter | solution.py:50
  29.0 0.8 copy-start
  138.1 13.9 %copy-start.2 = (f32[128,64]{0,1:T(8,128)}, f32[128,64]{0,1:T(8,128)S(1)}, u32[]{:S(2)}) copy-start(f32[128,64]{0,1:T(8,128)S(1)} %convolution_subtract_fusion) | copy-start | bytes 98308
Sparse Core Ops, SparseCore 0:
  43.2 19.8 reduce-scatter.1
where the time goes:
time: 160 us
  blocking collectives  94.3 us (59%)
  other arithmetic  25.2 us (16%)
  waiting for transfers between devices  19.9 us (12%)
  between operations  14.2 us (9%)
  matrix products  5.2 us (3%)
    psum x1, blocking collectives, local(): lax.psum((local_gram, local_curv, local_quad), ('blk', 'panel'))  60.6 us
    reduce_scatter x1, waiting for transfers between devices, local(): lax.psum_scatter(partial_value, 'panel', scatter_dimension=0, tiled=True)  19.8 us
    all_gather x1, blocking collectives, local(): lax.all_gather(points, 'blk', axis=0, tiled=True)  15.8 us
    another operation x6, other arithmetic, solve_spd(): jnp.linalg.cholesky(matrix)  13 us
    all_gather x1, blocking collectives, local(): lax.all_gather(dir_low, 'blk', axis=0, tiled=True)  12.1 us
    another operation x4, other arithmetic, solve_spd(): jax.scipy.linalg.cho_solve((jnp.linalg.cholesky(matrix), True), right)  11.1 us
    all_gather x1, blocking collectives, local(): queries = lax.all_gather(points, 'panel', axis=0, tiled=True)  5.77 us
  transfers between devices with their start and end apart: 1, of which 1 were waited for; matrix products, arithmetic and copies ran while one was open for 0% of the time, Pallas kernels for 0%

commit v1 on v0

v1 whole, which is shorter than its diff:
```python
import functools

import jax
import jax.numpy as jnp
from jax import lax
from jax.experimental import pallas as pl
from jax.experimental.pallas import tpu as pltpu
from jax.sharding import PartitionSpec as P

MESH = pl.DeviceIdType.MESH
HIGHEST = lax.Precision.HIGHEST
STEP = 8


def each(count, body):
    if count <= 8:
        for offset in range(1, count):
            body(offset)
    else:
        lax.fori_loop(1, count, lambda offset, carry: (body(offset), carry)[1], 0)


def dot_nt(a, b, precision=None):
    return lax.dot_general(
        a, b, (((1,), (1,)), ((), ())), precision=precision, preferred_element_type=jnp.float32
    )


def dot(a, b, precision=HIGHEST):
    return jnp.dot(a, b, precision=precision, preferred_element_type=jnp.float32)


def eliminate(whole, rows):
    width = whole.shape[1]
    blocks = [whole[i : i + STEP, :] for i in range(0, rows, STEP)]
    sub = lax.broadcasted_iota(jnp.int32, (STEP, width), 0)
    for k in range(rows // STEP):
        lead = blocks[k]
        spread = [
            [
                jnp.broadcast_to(block[:, k * STEP + j : k * STEP + j + 1], (STEP, width))
                for j in range(STEP)
            ]
            for block in blocks
        ]
        cols = list(spread[k])
        scales = jnp.ones((STEP, width), jnp.float32)
        for j in range(STEP):
            inverse = 1.0 / jnp.broadcast_to(cols[j][j : j + 1, :], (STEP, width))
            factor = jnp.where(sub == j, 0.0, cols[j] * inverse)
            scales = jnp.where(sub == j, inverse, scales)
            lead = lead - factor * jnp.broadcast_to(lead[j : j + 1, :], (STEP, width))
            for i in range(j + 1, STEP):
                cols[i] = cols[i] - factor * jnp.broadcast_to(cols[i][j : j + 1, :], (STEP, width))
        lead = lead * scales
        lead_rows = [jnp.broadcast_to(lead[j : j + 1, :], (STEP, width)) for j in range(STEP)]
        for i in range(rows // STEP):
            if i == k:
                blocks[i] = lead
            else:
                total = spread[i][0] * lead_rows[0]
                for j in range(1, STEP):
                    total = total + spread[i][j] * lead_rows[j]
                blocks[i] = blocks[i] - total
    return jnp.concatenate(blocks, axis=0)


def kernel(
    panels,
    blks,
    points_ref,
    targets_ref,
    solution_ref,
    residual_ref,
    direction_ref,
    queries,
    keys,
    dirs,
    parts,
    part_in,
    gram_own,
    gram_part,
    gram_chunk,
    gram_sum,
    small_own,
    small_part,
    small_chunk,
    small_sum,
    gram_inv,
    query_sems,
    key_sems,
    dir_sems,
    part_sems,
    gram_sems_part,
    gram_sems_chunk,
    gram_sems_sum,
    small_sems_part,
    small_sems_chunk,
    small_sems_sum,
):
    rows, depth = points_ref.shape
    wide_cols = targets_ref.shape[1]
    my_panel = lax.axis_index("panel")
    my_blk = lax.axis_index("blk")
    scale = 2.0 / depth

    def panel_at(offset):
        return {"panel": lax.rem(my_panel + offset, panels)}

    def blk_at(offset):
        return {"blk": lax.rem(my_blk + offset, blks)}

    def send(source, target, sems, index, device):
        return pltpu.make_async_remote_copy(
            src_ref=source,
            dst_ref=target,
            send_sem=sems.at[0, index],
            recv_sem=sems.at[1, index],
            device_id=device,
            device_id_type=MESH,
        )

    barrier = pltpu.get_barrier_semaphore()
    each(panels, lambda d: pl.semaphore_signal(barrier, inc=1, device_id=panel_at(d), device_id_type=MESH))
    each(blks, lambda d: pl.semaphore_signal(barrier, inc=1, device_id=blk_at(d), device_id_type=MESH))

    targets = targets_ref[...]
    targets_t = targets.T
    keys[0] = points_ref[...]
    queries[0] = points_ref[...]
    dirs[0] = targets_t.astype(jnp.bfloat16)
    double = jnp.concatenate([targets_t, targets_t], axis=0)
    gram_own[...] = dot_nt(targets_t, double, HIGHEST)
    pl.semaphore_wait(barrier, panels - 1 + blks - 1)

    def copy_query(d):
        return send(queries.at[0], queries.at[d], query_sems, d, panel_at(d))

    def copy_key(d):
        return send(keys.at[0], keys.at[d], key_sems, d, blk_at(d))

    def copy_dir(d):
        return send(dirs.at[0], dirs.at[d], dir_sems, d, blk_at(d))

    chunk = wide_cols // panels
    my_rows = pl.ds(pl.multiple_of(my_panel * chunk, 8), chunk)

    def scatter_copy(own, part, sems, d):
        owner = lax.rem(my_panel + d, panels)
        there = pl.ds(pl.multiple_of(owner * chunk, 8), chunk)
        return send(own.at[there, :], part.at[d], sems, d, panel_at(d))

    def scatter_start(own, part, sems):
        each(panels, lambda d: scatter_copy(own, part, sems, d).start())

    def exchange_copy(chunks, sems, d):
        return send(chunks.at[0], chunks.at[d], sems, d, blk_at(d))

    def exchange_start(own, part, sems, chunks, chunk_sems):
        each(panels, lambda d: scatter_copy(own, part, sems, d).wait())
        part[0] = own[my_rows, :]
        chunks[0] = jnp.sum(part[...], axis=0)
        each(blks, lambda d: exchange_copy(chunks, chunk_sems, d).start())

    def gather_copy(result, sems, d):
        return send(result.at[my_rows, :], result.at[my_rows, :], sems, d, panel_at(d))

    def gather_start(chunks, chunk_sems, result, sems):
        each(blks, lambda d: exchange_copy(chunks, chunk_sems, d).wait())
        result[my_rows, :] = jnp.sum(chunks[...], axis=0)
        each(panels, lambda d: gather_copy(result, sems, d).start())

    def gather_wait(result, sems):
        def one(d):
            back = lax.rem(my_panel + panels - d, panels)
            there = pl.ds(pl.multiple_of(back * chunk, 8), chunk)
            gather_copy(result, sems, d).wait_send()
            send(result.at[there, :], result.at[there, :], sems, d, panel_at(d)).wait_recv()

        each(panels, one)

    scatter_start(gram_own, gram_part, gram_sems_part)
    each(blks, lambda d: copy_key(d).start())
    each(blks, lambda d: copy_dir(d).start())
    each(panels, lambda d: copy_query(d).start())

    exchange_start(gram_own, gram_part, gram_sems_part, gram_chunk, gram_sems_chunk)
    gather_start(gram_chunk, gram_sems_chunk, gram_sum, gram_sems_sum)

    each(panels, lambda d: copy_query(d).wait())
    all_queries = queries[...].reshape(panels * rows, depth)
    wide = all_queries.astype(jnp.float32)
    sq_queries = dot_nt(jnp.full((8, depth), scale, jnp.float32), wide * wide, HIGHEST)[0:1, :]

    def tile(d):
        key = keys[d]
        wide_key = key.astype(jnp.float32)
        sq_key = jnp.sum(wide_key * wide_key, axis=1, keepdims=True) * scale
        cross = dot_nt(key, all_queries)
        weight = jnp.exp(jnp.minimum((2.0 * scale) * cross - sq_key - sq_queries, 0.0)).astype(jnp.bfloat16)
        return jnp.dot(dirs[d], weight, preferred_element_type=jnp.float32)

    first = tile(0)
    for p in range(panels):
        parts[p] = first[:, p * rows : (p + 1) * rows]

    gather_wait(gram_sum, gram_sems_sum)
    lane = lax.broadcasted_iota(jnp.int32, (wide_cols, 2 * wide_cols), 1)
    line = lax.broadcasted_iota(jnp.int32, (wide_cols, 2 * wide_cols), 0)
    gram2 = gram_sum[...]
    unit = (lane == line + wide_cols).astype(jnp.float32)
    gram_inv[...] = eliminate(jnp.where(lane < wide_cols, gram2, unit), wide_cols)

    def more(d):
        copy_key(d).wait()
        copy_dir(d).wait()
        value = tile(d)
        for p in range(panels):
            parts[p] += value[:, p * rows : (p + 1) * rows]

    each(blks, more)

    def copy_part(d):
        return send(parts.at[d], part_in.at[d], part_sems, d, panel_at(panels - d))

    each(panels, lambda d: copy_part(d).start())
    each(panels, lambda d: copy_part(d).wait())
    part_in[0] = parts[0]
    image_t = 1.0 * targets_t + jnp.sum(part_in[...], axis=0)
    small_own[...] = dot_nt(image_t, jnp.concatenate([targets_t, image_t], axis=0), HIGHEST)
    scatter_start(small_own, small_part, small_sems_part)
    both = jnp.concatenate([targets, image_t.T], axis=0)
    exchange_start(small_own, small_part, small_sems_part, small_chunk, small_sems_chunk)
    gather_start(small_chunk, small_sems_chunk, small_sum, small_sems_sum)
    gather_wait(small_sum, small_sems_sum)

    small = small_sum[...]
    curv_t = small[:, :wide_cols]
    quad = small[:, wide_cols:]
    curv = curv_t.T
    symmetric = 0.5 * (curv + curv_t)
    start = jnp.where(lane < wide_cols, jnp.concatenate([symmetric, symmetric], axis=1), gram2)
    alpha = eliminate(start, wide_cols)[:, wide_cols:]
    gram = gram2[:, :wide_cols]
    inner = dot(jnp.concatenate([quad, curv], axis=0), alpha)
    newgram = gram - inner[wide_cols:] + dot(alpha.T, inner[:wide_cols] - curv_t)
    made = dot(both, alpha)
    residual = targets - made[rows:]
    solution_ref[...] = made[:rows]
    residual_ref[...] = residual
    beta = dot(gram_inv[:, wide_cols:], newgram)
    direction_ref[...] = residual + dot(targets, beta)


def solution(mesh):
    panels, blks = mesh.shape["panel"], mesh.shape["blk"]

    def local(points, targets):
        rows, depth = points.shape
        cols = targets.shape[1]
        chunk = cols // panels
        f32, bf16 = jnp.float32, jnp.bfloat16
        out = jax.ShapeDtypeStruct((rows, cols), f32)
        vmem = pl.BlockSpec(memory_space=pltpu.VMEM)
        small = [
            pltpu.VMEM((cols, 2 * cols), f32),
            pltpu.VMEM((panels, chunk, 2 * cols), f32),
            pltpu.VMEM((blks, chunk, 2 * cols), f32),
            pltpu.VMEM((cols, 2 * cols), f32),
        ]
        panel_sems = pltpu.SemaphoreType.DMA((2, panels))
        blk_sems = pltpu.SemaphoreType.DMA((2, blks))
        return pl.pallas_call(
            functools.partial(kernel, panels, blks),
            out_shape=(out, out, out),
            in_specs=[vmem, vmem],
            out_specs=(vmem, vmem, vmem),
            scratch_shapes=[
                pltpu.VMEM((panels, rows, depth), bf16),
                pltpu.VMEM((blks, rows, depth), bf16),
                pltpu.VMEM((blks, cols, rows), bf16),
                pltpu.VMEM((panels, cols, rows), f32),
                pltpu.VMEM((panels, cols, rows), f32),
                *small,
                *small,
                pltpu.VMEM((cols, 2 * cols), f32),
                panel_sems,
                blk_sems,
                blk_sems,
                panel_sems,
                panel_sems,
                blk_sems,
                panel_sems,
                panel_sems,
                blk_sems,
                panel_sems,
            ],
            compiler_params=pltpu.CompilerParams(
                collective_id=0, has_side_effects=True, vmem_limit_bytes=48 * 1024 * 1024
            ),
        )(points, targets)

    placed = P(("groups", "blk", "panel"), None)
    return jax.shard_map(
        local,
        mesh=mesh,
        in_specs=(placed, placed),
        out_specs=(placed, placed, placed),
        check_vma=False,
    )
```

time: 160 us -> 40.1 us (0.25)
  blocking collectives: 94.3 us -> 0 us
  Pallas kernels: 0 us -> 36.3 us
  other arithmetic: 25.2 us -> 0 us
  waiting for transfers between devices: 19.9 us -> 0 us
  between operations: 14.2 us -> 0.66 us
  matrix products: 5.2 us -> 0 us
  local copies, waits for them, and re-layouts: 0.85 us -> 2.98 us
    psum x1 -> x0, blocking collectives: 60.6 us -> none  [local(): lax.psum((local_gram, local_curv, local_quad), ('blk', 'panel'))]
    pallas_call x0 -> x1, Pallas kernels: none -> 36.3 us  [local(): pl.pallas_call(functools.partial(kernel, panels, blks), out_shape=(out, o...]
    all_gather x3 -> x0, blocking collectives: 33.7 us -> none  [the longest x1 15.8 us: local(): lax.all_gather(points, 'blk', axis=0, tiled=True)]
    another operation x10 -> x0, other arithmetic: 24.1 us -> none  [the longest x6 13 us: solve_spd(): jnp.linalg.cholesky(matrix)]
    reduce_scatter x1 -> x0, waiting for transfers between devices: 19.8 us -> none  [local(): lax.psum_scatter(partial_value, 'panel', scatter_dimension=0, tiled=True)]
    dot_general x10 -> x0, matrix products: 4.4 us -> none  [the longest x1 1.26 us: one_block(): return jnp.dot(tile, dir_piece, preferred_element_type=jnp.float32)]
    pallas_call x0 -> x3, local copies, waits for them, and re-layouts: none -> 2.09 us  [local(): pl.pallas_call(functools.partial(kernel, panels, blks), out_shape=(out, o...]
  transfers between devices with their start and end apart: 1 -> 0, of which waited for: 1 -> 0; matrix products, arithmetic and copies ran while one was open for 0% -> 0% of each run, Pallas kernels for 0% -> 0%
where the time goes in v1:
time: 40.1 us; the launch traced here: 39.9 us
  Pallas kernels  36.3 us (91%)
  local copies, waits for them, and re-layouts  2.98 us (7%)
  between operations  0.66 us (2%)
    pallas_call x1, Pallas kernels, local(): pl.pallas_call(functools.partial(kernel, panels, blks), out_shape=(out, o...  36.3 us
    pallas_call x3, local copies, waits for them, and re-layouts, local(): pl.pallas_call(functools.partial(kernel, panels, blks), out_shape=(out, o...  2.09 us
    unnamed x3, local copies, waits for them, and re-layouts  0.88 us

profile of v1, /device:TPU:0, one launch (start us, length us, event | category | flops | bytes accessed | tf_op | source)
XLA Modules:
  0.0 39.9 jit_solution(9558474162596827656)
XLA Ops:
  0.6 0.0 copy-start
  0.6 0.9 %copy.5.targets_ref = f32[128,64]{1,0:T(8,128)S(1)} copy(f32[128,64]{0,1:T(8,128)} %param.3) | data formatting | bytes 65536 | tf_op args[1]
  1.5 0.0 copy-done
  1.5 36.3 %shard_map.49 = (f32[128,64]{1,0:T(8,128)S(1)}, f32[128,64]{1,0:T(8,128)S(1)}, f32[128,64]{1,0:T(8,128)S(1)}) custom-call(bf16[128,256]{1,0:T(8,128)(2,1)S(1)} %copy-done, f32[128,64]{1,0:T(8,128)S(1)} %copy.5.targets_ref), custom_call_target="tpu_custom_call" | custom-call | tf_op jit(solution)/shard_map/pallas_call | solution.py:273
  37.8 0.7 %copy.6 = f32[128,64]{0,1:T(8,128)} copy(f32[128,64]{1,0:T(8,128)S(1)} %get-tuple-element.3) | data formatting | bytes 65536 | tf_op jit(solution)/shard_map/pallas_call | solution.py:273
  38.5 0.7 %copy.7 = f32[128,64]{0,1:T(8,128)} copy(f32[128,64]{1,0:T(8,128)S(1)} %get-tuple-element.4) | data formatting | bytes 65536 | tf_op jit(solution)/shard_map/pallas_call | solution.py:273
  39.2 0.7 %copy.8 = f32[128,64]{0,1:T(8,128)} copy(f32[128,64]{1,0:T(8,128)S(1)} %get-tuple-element.5) | data formatting | bytes 65536 | tf_op jit(solution)/shard_map/pallas_call | solution.py:273
Async XLA Ops:
  0.6 0.9 %copy-start = (bf16[128,256]{1,0:T(8,128)(2,1)S(1)}, bf16[128,256]{1,0:T(8,128)(2,1)}, u32[]{:S(2)}) copy-start(bf16[128,256]{1,0:T(8,128)(2,1)} %points_ref.1) | copy-start | bytes 196612

commit v2 on v1

--- a/solution.py
+++ b/solution.py
@@ -86,7 +86,7 @@
     small_part,
     small_chunk,
     small_sum,
-    gram_inv,
+    solved,
     query_sems,
     key_sems,
     dir_sems,
@@ -99,7 +99,7 @@
     small_sems_sum,
 ):
     rows, depth = points_ref.shape
-    wide_cols = targets_ref.shape[1]
+    wide_cols = targets_ref.shape[0]
     my_panel = lax.axis_index("panel")
     my_blk = lax.axis_index("blk")
     scale = 2.0 / depth
@@ -124,8 +124,7 @@
     each(panels, lambda d: pl.semaphore_signal(barrier, inc=1, device_id=panel_at(d), device_id_type=MESH))
     each(blks, lambda d: pl.semaphore_signal(barrier, inc=1, device_id=blk_at(d), device_id_type=MESH))
 
-    targets = targets_ref[...]
-    targets_t = targets.T
+    targets_t = targets_ref[...]
     keys[0] = points_ref[...]
     queries[0] = points_ref[...]
     dirs[0] = targets_t.astype(jnp.bfloat16)
@@ -204,13 +203,6 @@
     for p in range(panels):
         parts[p] = first[:, p * rows : (p + 1) * rows]
 
-    gather_wait(gram_sum, gram_sems_sum)
-    lane = lax.broadcasted_iota(jnp.int32, (wide_cols, 2 * wide_cols), 1)
-    line = lax.broadcasted_iota(jnp.int32, (wide_cols, 2 * wide_cols), 0)
-    gram2 = gram_sum[...]
-    unit = (lane == line + wide_cols).astype(jnp.float32)
-    gram_inv[...] = eliminate(jnp.where(lane < wide_cols, gram2, unit), wide_cols)
-
     def more(d):
         copy_key(d).wait()
         copy_dir(d).wait()
@@ -224,32 +216,38 @@
         return send(parts.at[d], part_in.at[d], part_sems, d, panel_at(panels - d))
 
     each(panels, lambda d: copy_part(d).start())
+    gather_wait(gram_sum, gram_sems_sum)
+    lane = lax.broadcasted_iota(jnp.int32, (wide_cols, 2 * wide_cols), 1)
+    line = lax.broadcasted_iota(jnp.int32, (wide_cols, 2 * wide_cols), 0)
+    gram2 = gram_sum[...]
+    unit = (lane == line + wide_cols).astype(jnp.float32)
+    gram_inv = eliminate(jnp.where(lane < wide_cols, gram2, unit), wide_cols)[:, wide_cols:]
+    solved[...] = dot(gram_inv, targets_t)
+
     each(panels, lambda d: copy_part(d).wait())
     part_in[0] = parts[0]
     image_t = 1.0 * targets_t + jnp.sum(part_in[...], axis=0)
     small_own[...] = dot_nt(image_t, jnp.concatenate([targets_t, image_t], axis=0), HIGHEST)
     scatter_start(small_own, small_part, small_sems_part)
-    both = jnp.concatenate([targets, image_t.T], axis=0)
+    both = jnp.concatenate([targets_t, image_t], axis=1)
     exchange_start(small_own, small_part, small_sems_part, small_chunk, small_sems_chunk)
     gather_start(small_chunk, small_sems_chunk, small_sum, small_sems_sum)
     gather_wait(small_sum, small_sems_sum)
 
     small = small_sum[...]
     curv_t = small[:, :wide_cols]
-    quad = small[:, wide_cols:]
     curv = curv_t.T
     symmetric = 0.5 * (curv + curv_t)
     start = jnp.where(lane < wide_cols, jnp.concatenate([symmetric, symmetric], axis=1), gram2)
-    alpha = eliminate(start, wide_cols)[:, wide_cols:]
+    alpha_t = eliminate(start, wide_cols)[:, wide_cols:].T
     gram = gram2[:, :wide_cols]
-    inner = dot(jnp.concatenate([quad, curv], axis=0), alpha)
-    newgram = gram - inner[wide_cols:] + dot(alpha.T, inner[:wide_cols] - curv_t)
-    made = dot(both, alpha)
-    residual = targets - made[rows:]
-    solution_ref[...] = made[:rows]
+    made = dot(alpha_t, both)
+    residual = targets_t - made[:, rows:]
+    solution_ref[...] = made[:, :rows]
     residual_ref[...] = residual
-    beta = dot(gram_inv[:, wide_cols:], newgram)
-    direction_ref[...] = residual + dot(targets, beta)
+    inner = dot(alpha_t, small)
+    newgram = gram - inner[:, :wide_cols] + dot_nt(inner[:, wide_cols:] - curv, alpha_t, HIGHEST)
+    direction_ref[...] = residual + dot(newgram, solved[...])
 
 
 def solution(mesh):
@@ -260,7 +258,7 @@
         cols = targets.shape[1]
         chunk = cols // panels
         f32, bf16 = jnp.float32, jnp.bfloat16
-        out = jax.ShapeDtypeStruct((rows, cols), f32)
+        out = jax.ShapeDtypeStruct((cols, rows), f32)
         vmem = pl.BlockSpec(memory_space=pltpu.VMEM)
         small = [
             pltpu.VMEM((cols, 2 * cols), f32),
@@ -270,7 +268,7 @@
         ]
         panel_sems = pltpu.SemaphoreType.DMA((2, panels))
         blk_sems = pltpu.SemaphoreType.DMA((2, blks))
-        return pl.pallas_call(
+        outs = pl.pallas_call(
             functools.partial(kernel, panels, blks),
             out_shape=(out, out, out),
             in_specs=[vmem, vmem],
@@ -283,7 +281,7 @@
                 pltpu.VMEM((panels, cols, rows), f32),
                 *small,
                 *small,
-                pltpu.VMEM((cols, 2 * cols), f32),
+                pltpu.VMEM((cols, rows), f32),
                 panel_sems,
                 blk_sems,
                 blk_sems,
@@ -298,7 +296,8 @@
             compiler_params=pltpu.CompilerParams(
                 collective_id=0, has_side_effects=True, vmem_limit_bytes=48 * 1024 * 1024
             ),
-        )(points, targets)
+        )(points, targets.T)
+        return tuple(value.T for value in outs)
 
     placed = P(("groups", "blk", "panel"), None)
     return jax.shard_map(

time: 40.1 us -> 37.4 us (0.933)
  Pallas kernels: 36.3 us -> 33.1 us
  local copies, waits for them, and re-layouts: 2.98 us -> 3.44 us
    pallas_call x1, Pallas kernels: 36.3 us -> 33.1 us  [local(): pl.pallas_call(functools.partial(kernel, panels, blks), out_shape=(out, o...]
    unnamed x3 -> x7, local copies, waits for them, and re-layouts: 0.88 us -> 3.44 us
    pallas_call x3 -> x0, local copies, waits for them, and re-layouts: 2.09 us -> none  [local(): pl.pallas_call(functools.partial(kernel, panels, blks), out_shape=(out, o...]
where the time goes in v2:
time: 37.4 us; the launch traced here: 37.2 us
  Pallas kernels  33.1 us (89%)
  local copies, waits for them, and re-layouts  3.44 us (9%)
  between operations  0.65 us (2%)
    pallas_call x1, Pallas kernels, local(): pl.pallas_call(functools.partial(kernel, panels, blks), out_shape=(out, o...  33.1 us
    unnamed x7, local copies, waits for them, and re-layouts  3.44 us

profile of v2, /device:TPU:0, one launch (start us, length us, event | category | flops | bytes accessed | tf_op | source)
XLA Modules:
  0.0 37.2 jit_solution(12405849236704234713)
XLA Ops:
  0.6 0.0 copy-start
  0.6 0.8 %copy-done = bf16[128,256]{1,0:T(8,128)(2,1)S(1)} copy-done((bf16[128,256]{1,0:T(8,128)(2,1)S(1)}, bf16[128,256]{1,0:T(8,128)(2,1)}, u32[]{:S(2)}) %copy-start) | copy-done | bytes 65560
  1.5 0.0 copy-start.1
  1.5 0.8 %copy-done.1 = f32[128,64]{0,1:T(8,128)S(1)} copy-done((f32[128,64]{0,1:T(8,128)S(1)}, f32[128,64]{0,1:T(8,128)}, u32[]{:S(2)}) %copy-start.1) | copy-done | bytes 32792
  2.2 33.1 %shard_map.49 = (f32[64,128]{1,0:T(8,128)S(1)}, f32[64,128]{1,0:T(8,128)S(1)}, f32[64,128]{1,0:T(8,128)S(1)}) custom-call(bf16[128,256]{1,0:T(8,128)(2,1)S(1)} %copy-done, f32[64,128]{1,0:T(8,128)S(1)} %bitcast.4), custom_call_target="tpu_custom_call" | custom-call | tf_op jit(solution)/shard_map/pallas_call | solution.py:271
  35.3 0.6 %copy.8 = f32[128,64]{0,1:T(8,128)} copy(f32[128,64]{0,1:T(8,128)S(1)} %bitcast.7) | data formatting | bytes 65536
  36.0 0.6 %copy.9 = f32[128,64]{0,1:T(8,128)} copy(f32[128,64]{0,1:T(8,128)S(1)} %bitcast.6) | data formatting | bytes 65536
  36.6 0.6 %copy.10 = f32[128,64]{0,1:T(8,128)} copy(f32[128,64]{0,1:T(8,128)S(1)} %bitcast.5) | data formatting | bytes 65536
Async XLA Ops:
  0.6 0.8 %copy-start = (bf16[128,256]{1,0:T(8,128)(2,1)S(1)}, bf16[128,256]{1,0:T(8,128)(2,1)}, u32[]{:S(2)}) copy-start(bf16[128,256]{1,0:T(8,128)(2,1)} %points_ref.1) | copy-start | bytes 196612
  1.5 0.8 %copy-start.1 = (f32[128,64]{0,1:T(8,128)S(1)}, f32[128,64]{0,1:T(8,128)}, u32[]{:S(2)}) copy-start(f32[128,64]{0,1:T(8,128)} %param.3) | copy-start | bytes 98308

commit v3 on v2

v3 whole, which is shorter than its diff:
```python
import functools

import jax
import jax.numpy as jnp
from jax import lax
from jax.experimental import pallas as pl
from jax.experimental.pallas import tpu as pltpu
from jax.sharding import PartitionSpec as P

MESH = pl.DeviceIdType.MESH
HIGHEST = lax.Precision.HIGHEST
STEP = 8


def each(count, body):
    if count <= 16:
        for offset in range(1, count):
            body(offset)
    else:
        lax.fori_loop(1, count, lambda offset, carry: (body(offset), carry)[1], 0)


def dot_nt(a, b, precision=None):
    return lax.dot_general(
        a, b, (((1,), (1,)), ((), ())), precision=precision, preferred_element_type=jnp.float32
    )


def dot(a, b, precision=HIGHEST):
    return jnp.dot(a, b, precision=precision, preferred_element_type=jnp.float32)


def eliminate(whole, rows):
    width = whole.shape[1]
    blocks = [whole[i : i + STEP, :] for i in range(0, rows, STEP)]
    sub = lax.broadcasted_iota(jnp.int32, (STEP, width), 0)
    for k in range(rows // STEP):
        lead = blocks[k]
        spread = [
            [
                jnp.broadcast_to(block[:, k * STEP + j : k * STEP + j + 1], (STEP, width))
                for j in range(STEP)
            ]
            for block in blocks
        ]
        cols = list(spread[k])
        scales = jnp.ones((STEP, width), jnp.float32)
        for j in range(STEP):
            inverse = 1.0 / jnp.broadcast_to(cols[j][j : j + 1, :], (STEP, width))
            factor = jnp.where(sub == j, 0.0, cols[j] * inverse)
            scales = jnp.where(sub == j, inverse, scales)
            lead = lead - factor * jnp.broadcast_to(lead[j : j + 1, :], (STEP, width))
            for i in range(j + 1, STEP):
                cols[i] = cols[i] - factor * jnp.broadcast_to(cols[i][j : j + 1, :], (STEP, width))
        lead = lead * scales
        lead_rows = [jnp.broadcast_to(lead[j : j + 1, :], (STEP, width)) for j in range(STEP)]
        for i in range(rows // STEP):
            if i == k:
                blocks[i] = lead
            else:
                total = spread[i][0] * lead_rows[0]
                for j in range(1, STEP):
                    total = total + spread[i][j] * lead_rows[j]
                blocks[i] = blocks[i] - total
    return jnp.concatenate(blocks, axis=0)


def pack(value):
    half = value.shape[0] // 2
    return jnp.concatenate([value[:half], value[half:]], axis=1)


def unpack(value):
    half = value.shape[1] // 2
    return jnp.concatenate([value[:, :half], value[:, half:]], axis=0)


def kernel(
    panels,
    blks,
    points_ref,
    targets_ref,
    solution_ref,
    residual_ref,
    direction_ref,
    queries,
    keys,
    dirs,
    heights,
    parts,
    part_in,
    gram_panel,
    gram_blk,
    curv_panel,
    curv_blk,
    quad_panel,
    quad_blk,
    query_sems,
    key_sems,
    dir_sems,
    height_sems,
    part_sems,
    gram_panel_sems,
    gram_blk_sems,
    curv_panel_sems,
    curv_blk_sems,
    quad_panel_sems,
    quad_blk_sems,
    load_sems,
):
    rows, depth = points_ref.shape
    cols = targets_ref.shape[0]
    my_panel = lax.axis_index("panel")
    my_blk = lax.axis_index("blk")
    scale = 2.0 / depth

    def panel_at(offset):
        return {"panel": lax.rem(my_panel + offset, panels)}

    def blk_at(offset):
        return {"blk": lax.rem(my_blk + offset, blks)}

    def send(source, target, sems, index, device):
        return pltpu.make_async_remote_copy(
            src_ref=source,
            dst_ref=target,
            send_sem=sems.at[0, index],
            recv_sem=sems.at[1, index],
            device_id=device,
            device_id_type=MESH,
        )

    def panel_copy(buffer, sems, d):
        return send(buffer.at[0], buffer.at[d], sems, d, panel_at(d))

    def blk_copy(buffer, sems, d):
        return send(buffer.at[0], buffer.at[d], sems, d, blk_at(d))

    def over_panel(value, buffer, sems):
        buffer[0] = value
        each(panels, lambda d: panel_copy(buffer, sems, d).start())

    def over_blk(panel_buffer, panel_sems, buffer, sems):
        each(panels, lambda d: panel_copy(panel_buffer, panel_sems, d).wait())
        buffer[0] = jnp.sum(panel_buffer[...], axis=0)
        each(blks, lambda d: blk_copy(buffer, sems, d).start())

    def summed(buffer, sems):
        each(blks, lambda d: blk_copy(buffer, sems, d).wait())
        return unpack(jnp.sum(buffer[...], axis=0))

    barrier = pltpu.get_barrier_semaphore()
    each(blks, lambda d: pl.semaphore_signal(barrier, inc=1, device_id=blk_at(d), device_id_type=MESH))
    each(panels, lambda d: pl.semaphore_signal(barrier, inc=1, device_id=panel_at(d), device_id_type=MESH))
    load_targets = pltpu.make_async_copy(targets_ref, heights.at[0], load_sems.at[0])
    load_points = pltpu.make_async_copy(points_ref, queries.at[0], load_sems.at[1])
    load_targets.start()
    load_points.start()
    load_targets.wait()
    targets_t = heights[0]
    dirs[0] = targets_t.astype(jnp.bfloat16)
    own_gram = pack(dot_nt(targets_t, targets_t, HIGHEST))
    load_points.wait()

    def key_copy(d):
        return send(queries.at[0], keys.at[d], key_sems, d, blk_at(d))

    pl.semaphore_wait(barrier, panels - 1 + blks - 1)
    each(blks, lambda d: key_copy(d).start())
    each(blks, lambda d: blk_copy(dirs, dir_sems, d).start())
    each(panels, lambda d: panel_copy(queries, query_sems, d).start())
    over_panel(own_gram, gram_panel, gram_panel_sems)
    each(panels, lambda d: panel_copy(heights, height_sems, d).start())

    each(panels, lambda d: panel_copy(queries, query_sems, d).wait())
    over_blk(gram_panel, gram_panel_sems, gram_blk, gram_blk_sems)
    all_queries = queries[...].reshape(panels * rows, depth)
    wide = all_queries.astype(jnp.float32)
    sq_queries = dot_nt(jnp.full((8, depth), scale, jnp.float32), wide * wide, HIGHEST)[0:1, :]

    def tile(key, dir_piece):
        wide_key = key.astype(jnp.float32)
        sq_key = jnp.sum(wide_key * wide_key, axis=1, keepdims=True) * scale
        cross = dot_nt(key, all_queries)
        weight = jnp.exp(jnp.minimum((2.0 * scale) * cross - sq_key - sq_queries, 0.0)).astype(jnp.bfloat16)
        return jnp.dot(dir_piece, weight, preferred_element_type=jnp.float32)

    first = tile(queries[0], dirs[0])
    for p in range(panels):
        parts[p] = first[:, p * rows : (p + 1) * rows]

    def more(d):
        key_copy(d).wait()
        blk_copy(dirs, dir_sems, d).wait()
        value = tile(keys[d], dirs[d])
        for p in range(panels):
            parts[p] += value[:, p * rows : (p + 1) * rows]

    each(blks, more)

    def part_copy(d):
        return send(parts.at[d], part_in.at[d], part_sems, d, panel_at(panels - d))

    each(panels, lambda d: part_copy(d).start())
    each(panels, lambda d: panel_copy(heights, height_sems, d).wait())
    own_curv = dot_nt(parts[0], heights[0], HIGHEST)
    for p in range(1, panels):
        own_curv = own_curv + dot_nt(parts[p], heights[p], HIGHEST)
    over_panel(pack(own_curv), curv_panel, curv_panel_sems)

    lane = lax.broadcasted_iota(jnp.int32, (cols, 2 * cols), 1)
    line = lax.broadcasted_iota(jnp.int32, (cols, 2 * cols), 0)
    gram = summed(gram_blk, gram_blk_sems)
    twice = jnp.concatenate([gram, gram], axis=1)
    unit = (lane == line + cols).astype(jnp.float32)
    gram_inv = eliminate(jnp.where(lane < cols, twice, unit), cols)[:, cols:]
    solved = dot(gram_inv, targets_t)

    each(panels, lambda d: part_copy(d).wait())
    part_in[0] = parts[0]
    image_t = 1.0 * targets_t + jnp.sum(part_in[...], axis=0)
    over_panel(pack(dot_nt(image_t, image_t, HIGHEST)), quad_panel, quad_panel_sems)
    over_blk(curv_panel, curv_panel_sems, curv_blk, curv_blk_sems)
    over_blk(quad_panel, quad_panel_sems, quad_blk, quad_blk_sems)
    curv_t = gram + summed(curv_blk, curv_blk_sems)
    curv = curv_t.T
    symmetric = 0.5 * (curv + curv_t)
    start = jnp.concatenate([symmetric, gram], axis=1)
    alpha_t = eliminate(start, cols)[:, cols:].T
    made = dot(alpha_t, jnp.concatenate([targets_t, image_t], axis=1))
    residual = targets_t - made[:, rows:]
    solution_ref[...] = made[:, :rows]
    residual_ref[...] = residual
    known = gram - dot(alpha_t, curv_t) - dot_nt(curv, alpha_t, HIGHEST)
    moved = dot(alpha_t.T, solved)
    base = residual + dot(known, solved)
    quad = summed(quad_blk, quad_blk_sems)
    direction_ref[...] = base + dot(alpha_t, dot(quad, moved))


def solution(mesh):
    panels, blks = mesh.shape["panel"], mesh.shape["blk"]

    def local(points, targets):
        rows, depth = points.shape
        cols = targets.shape[1]
        f32, bf16 = jnp.float32, jnp.bfloat16
        out = jax.ShapeDtypeStruct((cols, rows), f32)
        vmem = pl.BlockSpec(memory_space=pltpu.VMEM)
        small = [pltpu.VMEM((panels, cols // 2, 2 * cols), f32), pltpu.VMEM((blks, cols // 2, 2 * cols), f32)]
        panel_sems = pltpu.SemaphoreType.DMA((2, panels))
        blk_sems = pltpu.SemaphoreType.DMA((2, blks))
        outs = pl.pallas_call(
            functools.partial(kernel, panels, blks),
            out_shape=(out, out, out),
            in_specs=[pl.BlockSpec(memory_space=pl.ANY)] * 2,
            out_specs=(vmem, vmem, vmem),
            scratch_shapes=[
                pltpu.VMEM((panels, rows, depth), bf16),
                pltpu.VMEM((blks, rows, depth), bf16),
                pltpu.VMEM((blks, cols, rows), bf16),
                pltpu.VMEM((panels, cols, rows), f32),
                pltpu.VMEM((panels, cols, rows), f32),
                pltpu.VMEM((panels, cols, rows), f32),
                *small,
                *small,
                *small,
                panel_sems,
                blk_sems,
                blk_sems,
                panel_sems,
                panel_sems,
                panel_sems,
                blk_sems,
                panel_sems,
                blk_sems,
                panel_sems,
                blk_sems,
                pltpu.SemaphoreType.DMA((2,)),
            ],
            compiler_params=pltpu.CompilerParams(collective_id=0, has_side_effects=True),
        )(points, targets.T)
        return tuple(value.T for value in outs)

    placed = P(("groups", "blk", "panel"), None)
    return jax.shard_map(
        local,
        mesh=mesh,
        in_specs=(placed, placed),
        out_specs=(placed, placed, placed),
        check_vma=False,
    )
```

time: 37.4 us -> 31.6 us (0.84)
  Pallas kernels: 33.1 us -> 27.9 us
  local copies, waits for them, and re-layouts: 3.44 us -> 2.77 us
    pallas_call x1, Pallas kernels: 33.1 us -> 27.9 us  [local(): pl.pallas_call(functools.partial(kernel, panels, blks), out_shape=(out, o...]
    unnamed x7, local copies, waits for them, and re-layouts: 3.44 us -> 2.77 us
where the time goes in v3:
time: 31.6 us; the launch traced here: 31.3 us
  Pallas kernels  27.9 us (88%)
  local copies, waits for them, and re-layouts  2.77 us (9%)
  between operations  0.65 us (2%)
    pallas_call x1, Pallas kernels, local(): pl.pallas_call(functools.partial(kernel, panels, blks), out_shape=(out, o...  27.9 us
    unnamed x7, local copies, waits for them, and re-layouts  2.77 us

profile of v3, /device:TPU:0, one launch (start us, length us, event | category | flops | bytes accessed | tf_op | source)
XLA Modules:
  0.0 31.3 jit_solution(5109392896930725087)
XLA Ops:
  0.6 27.9 %shard_map.49 = (f32[64,128]{1,0:T(8,128)}, f32[64,128]{1,0:T(8,128)}, f32[64,128]{1,0:T(8,128)}) custom-call(bf16[128,256]{1,0:T(8,128)(2,1)} %points_ref.1, f32[64,128]{1,0:T(8,128)} %bitcast.4), custom_call_target="tpu_custom_call" | custom-call | tf_op jit(solution)/shard_map/pallas_call | solution.py:253
  28.5 0.0 copy-start.1
  28.5 1.4 %copy.8 = f32[128,64]{0,1:T(8,128)} copy(f32[128,64]{0,1:T(8,128)} %bitcast.7) | data formatting | bytes 65536
  29.9 0.0 copy-done.1
  29.9 0.0 copy-start
  29.9 0.6 %copy.9 = f32[128,64]{0,1:T(8,128)} copy(f32[128,64]{0,1:T(8,128)S(1)} %bitcast.6) | data formatting | bytes 65536
  30.5 0.2 copy-done
  30.7 0.6 %copy.10 = f32[128,64]{0,1:T(8,128)} copy(f32[128,64]{0,1:T(8,128)S(1)} %bitcast.5) | data formatting | bytes 65536
Async XLA Ops:
  28.5 1.4 %copy-start.1 = (f32[64,128]{1,0:T(8,128)S(1)}, f32[64,128]{1,0:T(8,128)}, u32[]{:S(2)}) copy-start(f32[64,128]{1,0:T(8,128)} %get-tuple-element.7) | copy-start | bytes 98308
  29.9 0.8 %copy-start = (f32[64,128]{1,0:T(8,128)S(1)}, f32[64,128]{1,0:T(8,128)}, u32[]{:S(2)}) copy-start(f32[64,128]{1,0:T(8,128)} %get-tuple-element.8) | copy-start | bytes 98308

commit v4 on v3

--- a/solution.py
+++ b/solution.py
@@ -173,7 +173,6 @@
     each(panels, lambda d: panel_copy(heights, height_sems, d).start())
 
     each(panels, lambda d: panel_copy(queries, query_sems, d).wait())
-    over_blk(gram_panel, gram_panel_sems, gram_blk, gram_blk_sems)
     all_queries = queries[...].reshape(panels * rows, depth)
     wide = all_queries.astype(jnp.float32)
     sq_queries = dot_nt(jnp.full((8, depth), scale, jnp.float32), wide * wide, HIGHEST)[0:1, :]
@@ -202,12 +201,18 @@
         return send(parts.at[d], part_in.at[d], part_sems, d, panel_at(panels - d))
 
     each(panels, lambda d: part_copy(d).start())
+    over_blk(gram_panel, gram_panel_sems, gram_blk, gram_blk_sems)
     each(panels, lambda d: panel_copy(heights, height_sems, d).wait())
     own_curv = dot_nt(parts[0], heights[0], HIGHEST)
     for p in range(1, panels):
         own_curv = own_curv + dot_nt(parts[p], heights[p], HIGHEST)
     over_panel(pack(own_curv), curv_panel, curv_panel_sems)
 
+    each(panels, lambda d: part_copy(d).wait())
+    part_in[0] = parts[0]
+    image_t = 1.0 * targets_t + jnp.sum(part_in[...], axis=0)
+    over_panel(pack(dot_nt(image_t, image_t, HIGHEST)), quad_panel, quad_panel_sems)
+    over_blk(curv_panel, curv_panel_sems, curv_blk, curv_blk_sems)
     lane = lax.broadcasted_iota(jnp.int32, (cols, 2 * cols), 1)
     line = lax.broadcasted_iota(jnp.int32, (cols, 2 * cols), 0)
     gram = summed(gram_blk, gram_blk_sems)
@@ -216,11 +221,6 @@
     gram_inv = eliminate(jnp.where(lane < cols, twice, unit), cols)[:, cols:]
     solved = dot(gram_inv, targets_t)
 
-    each(panels, lambda d: part_copy(d).wait())
-    part_in[0] = parts[0]
-    image_t = 1.0 * targets_t + jnp.sum(part_in[...], axis=0)
-    over_panel(pack(dot_nt(image_t, image_t, HIGHEST)), quad_panel, quad_panel_sems)
-    over_blk(curv_panel, curv_panel_sems, curv_blk, curv_blk_sems)
     over_blk(quad_panel, quad_panel_sems, quad_blk, quad_blk_sems)
     curv_t = gram + summed(curv_blk, curv_blk_sems)
     curv = curv_t.T
@@ -236,6 +236,11 @@
     base = residual + dot(known, solved)
     quad = summed(quad_blk, quad_blk_sems)
     direction_ref[...] = base + dot(alpha_t, dot(quad, moved))
+
+
+def write(solution_ref, residual_ref, direction_ref, *outs):
+    for source, out in zip((solution_ref, residual_ref, direction_ref), outs):
+        out[...] = source[...]
 
 
 def solution(mesh):
@@ -280,7 +285,8 @@
             ],
             compiler_params=pltpu.CompilerParams(collective_id=0, has_side_effects=True),
         )(points, targets.T)
-        return tuple(value.T for value in outs)
+        done = pl.pallas_call(write, out_shape=(out, out, out), in_specs=[vmem] * 3, out_specs=(vmem,) * 3)(*outs)
+        return tuple(value.T for value in done)
 
     placed = P(("groups", "blk", "panel"), None)
     return jax.shard_map(

time: 31.6 us -> 29.1 us (0.921)
  local copies, waits for them, and re-layouts: 2.77 us -> 0 us
    unnamed x7 -> x0, local copies, waits for them, and re-layouts: 2.77 us -> none
    pallas_call x0 -> x1, Pallas kernels: none -> 1.43 us  [local(): pl.pallas_call(write, out_shape=(out, out, out), in_specs=[vmem] * 3, out...]
    pallas_call x1, Pallas kernels: 27.9 us -> 26.8 us  [local(): pl.pallas_call(functools.partial(kernel, panels, blks), out_shape=(out, o...]
where the time goes in v4:
time: 29.1 us; the launch traced here: 28.9 us
  Pallas kernels  28.2 us (97%)
  between operations  0.64 us (2%)
    pallas_call x1, Pallas kernels, local(): pl.pallas_call(functools.partial(kernel, panels, blks), out_shape=(out, o...  26.8 us
    pallas_call x1, Pallas kernels, local(): pl.pallas_call(write, out_shape=(out, out, out), in_specs=[vmem] * 3, out...  1.43 us

profile of v4, /device:TPU:0, one launch (start us, length us, event | category | flops | bytes accessed | tf_op | source)
XLA Modules:
  0.0 28.9 jit_solution(14092459384735174663)
XLA Ops:
  0.6 26.8 %shard_map.49 = (f32[64,128]{1,0:T(8,128)}, f32[64,128]{1,0:T(8,128)}, f32[64,128]{1,0:T(8,128)}) custom-call(bf16[128,256]{1,0:T(8,128)(2,1)} %points_ref.1, f32[64,128]{1,0:T(8,128)} %bitcast.4), custom_call_target="tpu_custom_call" | custom-call | tf_op jit(solution)/shard_map/pallas_call | solution.py:258
  27.4 1.4 %shard_map.50 = (f32[64,128]{1,0:T(8,128)}, f32[64,128]{1,0:T(8,128)}, f32[64,128]{1,0:T(8,128)}) custom-call(f32[64,128]{1,0:T(8,128)} %get-tuple-element.9.solution_ref, f32[64,128]{1,0:T(8,128)} %get-tuple-element.10.residual_ref, f32[64,128]{1,0:T(8,128)} %get-tuple-element.11.direction_ref), custom_call_target="tpu_custom_call" | custom-call | tf_op jit(solution)/shard_map/pallas_call | solution.py:288

commit v5 on v4

--- a/solution.py
+++ b/solution.py
@@ -226,16 +226,17 @@
     curv = curv_t.T
     symmetric = 0.5 * (curv + curv_t)
     start = jnp.concatenate([symmetric, gram], axis=1)
-    alpha_t = eliminate(start, cols)[:, cols:].T
+    alpha = eliminate(start, cols)[:, cols:]
+    alpha_t = alpha.T
+    moved = dot(alpha, solved)
+    quad = summed(quad_blk, quad_blk_sems)
+    squared = dot(alpha_t, dot(quad, moved))
     made = dot(alpha_t, jnp.concatenate([targets_t, image_t], axis=1))
     residual = targets_t - made[:, rows:]
+    known = gram - dot(alpha_t, curv_t) - dot_nt(curv, alpha_t, HIGHEST)
     solution_ref[...] = made[:, :rows]
     residual_ref[...] = residual
-    known = gram - dot(alpha_t, curv_t) - dot_nt(curv, alpha_t, HIGHEST)
-    moved = dot(alpha_t.T, solved)
-    base = residual + dot(known, solved)
-    quad = summed(quad_blk, quad_blk_sems)
-    direction_ref[...] = base + dot(alpha_t, dot(quad, moved))
+    direction_ref[...] = residual + dot(known, solved) + squared
 
 
 def write(solution_ref, residual_ref, direction_ref, *outs):

time: 29.1 us -> 29.1 us (level)
  no operation moved by 1% of the time
where the time goes in v5:
time: 29.1 us; the launch traced here: 28.8 us
  Pallas kernels  28.2 us (97%)
  between operations  0.64 us (2%)
    pallas_call x1, Pallas kernels, local(): pl.pallas_call(functools.partial(kernel, panels, blks), out_shape=(out, o...  26.8 us
    pallas_call x1, Pallas kernels, local(): pl.pallas_call(write, out_shape=(out, out, out), in_specs=[vmem] * 3, out...  1.43 us

profile of v5, /device:TPU:0, one launch (start us, length us, event | category | flops | bytes accessed | tf_op | source)
XLA Modules:
  0.0 28.8 jit_solution(16226622929918567424)
XLA Ops:
  0.6 26.8 %shard_map.49 = (f32[64,128]{1,0:T(8,128)}, f32[64,128]{1,0:T(8,128)}, f32[64,128]{1,0:T(8,128)}) custom-call(bf16[128,256]{1,0:T(8,128)(2,1)} %points_ref.1, f32[64,128]{1,0:T(8,128)} %bitcast.4), custom_call_target="tpu_custom_call" | custom-call | tf_op jit(solution)/shard_map/pallas_call | solution.py:259
  27.4 1.4 %shard_map.50 = (f32[64,128]{1,0:T(8,128)}, f32[64,128]{1,0:T(8,128)}, f32[64,128]{1,0:T(8,128)}) custom-call(f32[64,128]{1,0:T(8,128)} %get-tuple-element.9.solution_ref, f32[64,128]{1,0:T(8,128)} %get-tuple-element.10.residual_ref, f32[64,128]{1,0:T(8,128)} %get-tuple-element.11.direction_ref), custom_call_target="tpu_custom_call" | custom-call | tf_op jit(solution)/shard_map/pallas_call | solution.py:289

commit v6 on v5

--- a/solution.py
+++ b/solution.py
@@ -239,9 +239,18 @@
     direction_ref[...] = residual + dot(known, solved) + squared
 
 
-def write(solution_ref, residual_ref, direction_ref, *outs):
-    for source, out in zip((solution_ref, residual_ref, direction_ref), outs):
-        out[...] = source[...]
+def write(solution_ref, residual_ref, direction_ref, solution_out, residual_out, direction_out, held, sems):
+    sources = (solution_ref, residual_ref, direction_ref)
+    outs = (solution_out, residual_out, direction_out)
+    loads = [pltpu.make_async_copy(source, held.at[i], sems.at[0, i]) for i, source in enumerate(sources)]
+    stores = [pltpu.make_async_copy(held.at[i], out, sems.at[1, i]) for i, out in enumerate(outs)]
+    for load in loads:
+        load.start()
+    for load, store in zip(loads, stores):
+        load.wait()
+        store.start()
+    for store in stores:
+        store.wait()
 
 
 def solution(mesh):
@@ -286,7 +295,13 @@
             ],
             compiler_params=pltpu.CompilerParams(collective_id=0, has_side_effects=True),
         )(points, targets.T)
-        done = pl.pallas_call(write, out_shape=(out, out, out), in_specs=[vmem] * 3, out_specs=(vmem,) * 3)(*outs)
+        done = pl.pallas_call(
+            write,
+            out_shape=(out, out, out),
+            in_specs=[pl.BlockSpec(memory_space=pl.ANY)] * 3,
+            out_specs=(pl.BlockSpec(memory_space=pl.ANY),) * 3,
+            scratch_shapes=[pltpu.VMEM((3, cols, rows), f32), pltpu.SemaphoreType.DMA((2, 3))],
+        )(*outs)
         return tuple(value.T for value in done)
 
     placed = P(("groups", "blk", "panel"), None)

time: 29.1 us -> 29.1 us (level)
  no operation moved by 1% of the time
where the time goes in v6:
time: 29.1 us; the launch traced here: 28.8 us
  Pallas kernels  28.2 us (97%)
  between operations  0.64 us (2%)
    pallas_call x1, Pallas kernels, local(): pl.pallas_call(functools.partial(kernel, panels, blks), out_shape=(out, o...  26.8 us
    pallas_call x1, Pallas kernels, local(): pl.pallas_call(write, out_shape=(out, out, out), in_specs=[pl.BlockSpec(m...  1.46 us

profile of v6, /device:TPU:0, one launch (start us, length us, event | category | flops | bytes accessed | tf_op | source)
XLA Modules:
  0.0 28.8 jit_solution(6671498197313408548)
XLA Ops:
  0.6 26.8 %shard_map.49 = (f32[64,128]{1,0:T(8,128)}, f32[64,128]{1,0:T(8,128)}, f32[64,128]{1,0:T(8,128)}) custom-call(bf16[128,256]{1,0:T(8,128)(2,1)} %points_ref.1, f32[64,128]{1,0:T(8,128)} %bitcast.4), custom_call_target="tpu_custom_call" | custom-call | tf_op jit(solution)/shard_map/pallas_call | solution.py:268
  27.4 1.5 %shard_map.50 = (f32[64,128]{1,0:T(8,128)}, f32[64,128]{1,0:T(8,128)}, f32[64,128]{1,0:T(8,128)}) custom-call(f32[64,128]{1,0:T(8,128)} %get-tuple-element.9.solution_ref, f32[64,128]{1,0:T(8,128)} %get-tuple-element.10.residual_ref, f32[64,128]{1,0:T(8,128)} %get-tuple-element.11.direction_ref), custom_call_target="tpu_custom_call" | custom-call | tf_op jit(solution)/shard_map/pallas_call | solution.py:298
